TPU v7x, 512 devices: a whole 4x4x16 slice. The times are simulated.
512 devices in a mesh: row: 16 (over z), col: 32 (over x, y, core).
Axes of the slice: x: 4, y: 4, z: 16, core: 2. Of those that a mesh axis runs over, the one named last changes fastest.
Arguments:
- latent: bfloat16 [4, 192, 256, 256], P(None, 'row', 'col'), may hold values from -32 to 32
- group_gain: float32 [256], replicated, may hold values from 0.1 to 1.9
- group_shift: float32 [256], replicated, may hold values from -3 to 3
- kernel: bfloat16 [27, 256, 256], replicated, may hold values from -0.078125 to 0.078125
- kernel_bias: float32 [256], replicated, may hold values from -3 to 3
Outputs:
- features: bfloat16 [4, 192, 256, 256], P(None, 'row', 'col')
All inputs are finite; a program needn't handle non-finite values.
Results may differ from a plain program's by a relative error of at most 0.0065.
Values may be sent and summed in bfloat16 or wider, within the bound.
A program may use at most 64 MiB of HBM per device.

v0:
```python
import jax
import jax.numpy as jnp
from jax import lax
from jax.sharding import PartitionSpec as P

GROUP_CH = 16


EPSILON = 1e-06


def extended(cells, sides, width):
    for axis, dim in sides:
        count = lax.axis_size(axis)
        ends = count - 1
        head = lax.slice_in_dim(cells, 0, width, axis=dim)
        tail = lax.slice_in_dim(cells, cells.shape[dim] - width, cells.shape[dim], axis=dim)
        cells = jnp.concatenate(
            [
                lax.ppermute(tail, axis, [(i, (i + 1) % count) for i in range(ends)]),
                cells,
                lax.ppermute(head, axis, [((i + 1) % count, i) for i in range(ends)]),
            ],
            axis=dim,
        )
    return cells


def body(latent, group_gain, group_shift, kernel, kernel_bias):
    frames, height, breadth, channels = latent.shape
    groups = channels // GROUP_CH
    member_count = (
        frames * height * breadth * GROUP_CH * lax.axis_size("row") * lax.axis_size("col")
    )
    values = latent.astype(jnp.float32).reshape(frames, height, breadth, groups, GROUP_CH)
    totals = lax.psum(jnp.sum(values, axis=(0, 1, 2, 4)), ("row", "col"))
    group_means = totals / member_count
    spread = values - group_means[:, None]
    squares = lax.psum(jnp.sum(spread * spread, axis=(0, 1, 2, 4)), ("row", "col"))
    variance = squares / member_count
    scaling = group_gain.reshape(groups, GROUP_CH) * lax.rsqrt(variance + EPSILON)[:, None]
    offsets = group_shift.reshape(groups, GROUP_CH) - group_means[:, None] * scaling
    scaling = scaling.reshape(channels)
    offsets = offsets.reshape(channels)
    bordered = extended(
        jax.nn.silu(latent.astype(jnp.float32) * scaling + offsets).astype(jnp.bfloat16),
        (("row", 1), ("col", 2)),
        1,
    )
    row_index = lax.axis_index("row")
    col_index = lax.axis_index("col")
    upper_rim = jnp.where(row_index == 0, bordered[:, 1:2], bordered[:, 0:1])
    lower_rim = jnp.where(
        row_index == lax.axis_size("row") - 1, bordered[:, -2:-1], bordered[:, -1:]
    )
    bordered = jnp.concatenate([upper_rim, bordered[:, 1:-1], lower_rim], axis=1)
    left_rim = jnp.where(col_index == 0, bordered[:, :, 1:2], bordered[:, :, 0:1])
    right_rim = jnp.where(
        col_index == lax.axis_size("col") - 1, bordered[:, :, -2:-1], bordered[:, :, -1:]
    )
    bordered = jnp.concatenate([left_rim, bordered[:, :, 1:-1], right_rim], axis=2)
    padded = jnp.concatenate([bordered[:1], bordered[:1], bordered], axis=0)
    accumulated = jnp.zeros((frames * height * breadth, channels), jnp.float32)
    for time_tap in range(3):
        for row_tap in range(3):
            for col_tap in range(3):
                window = padded[
                    time_tap : time_tap + frames,
                    row_tap : row_tap + height,
                    col_tap : col_tap + breadth,
                ]
                window = window.reshape(frames * height * breadth, channels)
                accumulated = accumulated + jnp.dot(
                    window,
                    kernel[9 * time_tap + 3 * row_tap + col_tap],
                    preferred_element_type=jnp.float32,
                )
    result = (accumulated + kernel_bias).astype(jnp.bfloat16)
    return result.reshape(frames, height, breadth, channels)


def solution(mesh):
    return jax.shard_map(
        body,
        mesh=mesh,
        in_specs=(P(None, "row", "col", None), P(), P(), P(), P()),
        out_specs=P(None, "row", "col", None),
        check_vma=False,
    )
```

profile of v0, /device:TPU:1, one launch (start us, length us, event | category | flops | bytes accessed | tf_op | source)
XLA Modules:
  0.0 238.0 jit_solution(9889780639874570239)
XLA Ops:
  0.0 1.0 convert_reduce_fusion
  1.0 0.1 reduce_sum.24
  1.1 0.1 reduce_sum.25
  1.2 111.0 %psum.14 = f32[16]{0:T(128)S(1)} all-reduce(f32[16]{0:T(128)S(1)} %reduce_sum.25), channel_id=1, replica_groups=mesh['row'=16,'col'=32] {'row','col'}, use_global_device_ids=true, to_apply=%region_2.0 | all-reduce | flops 16 | bytes 128 | tf_op jit(solution)/shard_map/psum | solution.py:36
  112.2 0.1 sub.18
  112.3 0.1 sub.19
  112.4 1.0 fusion.3
  113.4 0.1 reduce_sum.36
  113.5 0.1 reduce_sum.37
  113.6 98.3 %psum.15 = f32[16]{0:T(128)S(1)} all-reduce(f32[16]{0:T(128)S(1)} %reduce_sum.37), channel_id=1, replica_groups=mesh['row'=16,'col'=32] {'row','col'}, use_global_device_ids=true, to_apply=%region_5.6 | all-reduce | flops 16 | bytes 128 | tf_op jit(solution)/shard_map/psum | solution.py:39
  211.9 0.1 mul.38
  212.0 0.1 mul.39
  212.1 0.7 multiply_subtract_fusion
  212.8 1.0 fusion.10
  213.8 1.3 collective-permute-start.1
  215.1 4.3 %collective-permute-start = (bf16[4,1,8,256]{3,2,1,0:T(8,128)(2,1)S(1)}, bf16[4,1,8,256]{3,2,1,0:T(8,128)(2,1)S(1)}, u32[]{:S(2)}, u32[]{:S(2)}) collective-permute-start(bf16[4,1,8,256]{3,2,1,0:T(8,128)(2,1)S(1)} %get-tuple-element.40), channel_id=1, source_target_pairs={{0,32},{32,64},{64,96},{96,128},{128,160},{160,192},{192,224},{224... | collective-permute-start | bytes 49160 | tf_op jit(solution)/shard_map/ppermute | solution.py:20
  219.4 0.0 collective-permute-done.1
  219.5 0.8 collective-permute-done
  220.3 0.1 pad_maximum_fusion.10
  220.4 3.4 %collective-permute-start.3 = (bf16[4,14,1,256]{3,2,1,0:T(2,128)(2,1)S(1)}, bf16[4,14,1,256]{3,2,1,0:T(2,128)(2,1)S(1)}, u32[]{:S(2)}, u32[]{:S(2)}) collective-permute-start(bf16[4,14,1,256]{3,2,1,0:T(2,128)(2,1)S(1)} %get-tuple-element.39), channel_id=1, source_target_pairs={{1,0},{2,1},{3,2},{4,3},{5,4},{6,5},{7,6},{8,7},{9,8},{10,9},{11,1... | collective-permute-start | bytes 86024 | tf_op jit(solution)/shard_map/ppermute | solution.py:22
  223.8 2.3 collective-permute-start.2
  226.2 0.0 collective-permute-done.3
  226.2 1.2 collective-permute-done.2
  227.4 0.3 pad_maximum_fusion
  227.8 0.1 pad_maximum_fusion.1
  227.9 0.1 slice.300
  228.0 0.2 broadcast_select_fusion.1
  228.1 0.1 pad_maximum_fusion.6
  228.2 0.3 maximum_maximum_fusion
  228.5 0.3 maximum_maximum_fusion.1
  228.8 0.5 pad_maximum_fusion.2
  229.3 0.1 pad_maximum_fusion.3
  229.4 0.0 copy-start
  229.4 0.2 fusion.70
  229.6 0.2 fusion.71
  229.8 1.6 copy-done
  231.4 0.2 fusion.41
  231.6 0.2 convolution_add_fusion.25
  231.8 0.2 convolution_add_fusion.24
  232.0 0.2 convolution_add_fusion.23
  232.2 0.2 convolution_add_fusion.22
  232.5 0.2 convolution_add_fusion.21
  232.7 0.2 convolution_add_fusion.20
  232.9 0.2 convolution_add_fusion.19
  233.1 0.2 convolution_add_fusion.18
  233.3 0.2 convolution_add_fusion.17
  233.6 0.2 convolution_add_fusion.16
  233.8 0.2 convolution_add_fusion.15
  234.0 0.2 convolution_add_fusion.14
  234.2 0.2 convolution_add_fusion.13
  234.4 0.2 convolution_add_fusion.12
  234.6 0.2 convolution_add_fusion.11
  234.9 0.2 convolution_add_fusion.10
  235.1 0.2 convolution_add_fusion.9
  235.3 0.2 convolution_add_fusion.8
  235.5 0.2 convolution_add_fusion.7
  235.7 0.0 copy-start.1
  235.8 0.2 convolution_add_fusion.6
  236.0 0.2 convolution_add_fusion.5
  236.2 0.2 convolution_add_fusion.4
  236.4 0.2 convolution_add_fusion.3
  236.6 0.2 convolution_add_fusion.2
  236.8 0.2 convolution_add_fusion.1
  237.1 0.9 fusion.1
  (7 shorter events, 0.1 us)
Async XLA Ops:
  213.8 5.6 %collective-permute-start.1 = (bf16[4,1,8,256]{3,2,1,0:T(8,128)(2,1)S(1)}, bf16[4,1,8,256]{3,2,1,0:T(8,128)(2,1)S(1)}, u32[]{:S(2)}, u32[]{:S(2)}) collective-permute-start(bf16[4,1,8,256]{3,2,1,0:T(8,128)(2,1)S(1)} %get-tuple-element.41), channel_id=1, source_target_pairs={{32,0},{64,32},{96,64},{128,96},{160,128},{192,160},{224,192},{256... | collective-permute-start | bytes 49160 | tf_op jit(solution)/shard_map/ppermute | solution.py:22
  215.1 5.2 %collective-permute-start = (bf16[4,1,8,256]{3,2,1,0:T(8,128)(2,1)S(1)}, bf16[4,1,8,256]{3,2,1,0:T(8,128)(2,1)S(1)}, u32[]{:S(2)}, u32[]{:S(2)}) collective-permute-start(bf16[4,1,8,256]{3,2,1,0:T(8,128)(2,1)S(1)} %get-tuple-element.40), channel_id=1, source_target_pairs={{0,32},{32,64},{64,96},{96,128},{128,160},{160,192},{192,224},{224... | collective-permute-start | bytes 49160 | tf_op jit(solution)/shard_map/ppermute | solution.py:20
  220.4 5.8 %collective-permute-start.3 = (bf16[4,14,1,256]{3,2,1,0:T(2,128)(2,1)S(1)}, bf16[4,14,1,256]{3,2,1,0:T(2,128)(2,1)S(1)}, u32[]{:S(2)}, u32[]{:S(2)}) collective-permute-start(bf16[4,14,1,256]{3,2,1,0:T(2,128)(2,1)S(1)} %get-tuple-element.39), channel_id=1, source_target_pairs={{1,0},{2,1},{3,2},{4,3},{5,4},{6,5},{7,6},{8,7},{9,8},{10,9},{11,1... | collective-permute-start | bytes 86024 | tf_op jit(solution)/shard_map/ppermute | solution.py:22
  223.8 3.6 %collective-permute-start.2 = (bf16[4,14,1,256]{3,2,1,0:T(2,128)(2,1)S(1)}, bf16[4,14,1,256]{3,2,1,0:T(2,128)(2,1)S(1)}, u32[]{:S(2)}, u32[]{:S(2)}) collective-permute-start(bf16[4,14,1,256]{3,2,1,0:T(2,128)(2,1)S(1)} %get-tuple-element.38), channel_id=1, source_target_pairs={{0,1},{1,2},{2,3},{3,4},{4,5},{5,6},{6,7},{7,8},{8,9},{9,10},{10,1... | collective-permute-start | bytes 86024 | tf_op jit(solution)/shard_map/ppermute | solution.py:20
  229.4 2.0 copy-start
  235.7 1.3 copy-start.1
where the time goes:
time: 242 us; the launch traced here: 238 us
  blocking collectives  209 us (86%)
  starting transfers between devices  11.4 us (5%)
  matrix products  6.37 us (3%)
  other arithmetic  5.9 us (2%)
  local copies, waits for them, and re-layouts  2.56 us (1%)
    psum x1, blocking collectives, body(): totals = lax.psum(jnp.sum(values, axis=(0, 1, 2, 4)), ('row', 'col'))  111 us
    psum x1, blocking collectives, body(): lax.psum(jnp.sum(spread * spread, axis=(0, 1, 2, 4)), ('row', 'col'))  98.3 us
    ppermute x2, starting transfers between devices, extended(): lax.ppermute(tail, axis, [(i, (i + 1) % count) for i in range(ends)])  6.64 us
    dot_general x27, matrix products, body(): jnp.dot(window, kernel[9 * time_tap + 3 * row_tap + col_tap], preferred_e...  6.37 us
  transfers between devices with their start and end apart: 4, of which 2 were waited for; matrix products, arithmetic and copies ran while one was open for 0% of the time, Pallas kernels for 0%

commit v1 on v0

v1 whole, which is shorter than its diff:
```python
import functools

import jax
import jax.numpy as jnp
from jax import lax
from jax.experimental import pallas as pl
from jax.experimental.pallas import tpu as pltpu
from jax.sharding import PartitionSpec as P

GROUP_CH = 16
EPSILON = 1e-06
MESH = pl.DeviceIdType.MESH
ROOT_ROW, ROOT_COL = 0, 1
F32 = jnp.float32


def group_total(values):
    lane = lax.broadcasted_iota(jnp.int32, values.shape, 1)
    for step in (1, 2, 4, 8):
        upper = (lane & step) != 0
        values = values + jnp.where(
            upper, pltpu.roll(values, step, 1), pltpu.roll(values, 128 - step, 1)
        )
    return values


def kernel(
    rows,
    cols,
    latent_hbm,
    gain_hbm,
    shift_hbm,
    weights_hbm,
    bias_hbm,
    out_ref,
    raw,
    gain_ref,
    shift_ref,
    bias_ref,
    weights,
    own,
    row_out,
    col_out,
    corner_out,
    row_in,
    col_in,
    corner_in,
    stat_row,
    gathered,
    params,
    windows,
    rims,
    patches,
    load_sem,
    halo_send,
    halo_recv,
    stat_send,
    stat_recv,
    param_send,
    param_recv,
):
    row, col = lax.axis_index("row"), lax.axis_index("col")
    devices = rows * cols
    me = row * cols + col
    is_root = jnp.logical_and(row == ROOT_ROW, col == ROOT_COL)
    up, down = lax.rem(row + rows - 1, rows), lax.rem(row + 1, rows)
    left, right = lax.rem(col + cols - 1, cols), lax.rem(col + 1, cols)

    load = pltpu.make_async_copy(latent_hbm, raw, load_sem.at[0])
    load.start()

    barrier = pltpu.get_barrier_semaphore()
    for r in (up, row, down):
        for c in (left, col, right):
            if r is not row or c is not col:
                pl.semaphore_signal(barrier, inc=1, device_id=(r, c), device_id_type=MESH)

    @pl.when(is_root)
    def _():
        def greet(i, carry):
            @pl.when(i != me)
            def _():
                pl.semaphore_signal(
                    barrier,
                    inc=1,
                    device_id=(lax.div(i, cols), lax.rem(i, cols)),
                    device_id_type=MESH,
                )

            return carry

        lax.fori_loop(0, devices, greet, 0)

    later = [
        pltpu.make_async_copy(source, target, load_sem.at[1 + i])
        for i, (source, target) in enumerate(
            (
                (gain_hbm, gain_ref),
                (shift_hbm, shift_ref),
                (bias_hbm, bias_ref),
                (weights_hbm, weights),
            )
        )
    ]
    for copy in later:
        copy.start()

    load.wait()
    values = raw[...].astype(F32)
    own[0] = values[:, :128]
    own[1] = values[:, 128:]
    count = values.shape[0]
    sums = jnp.sum(values, axis=0, keepdims=True)
    means = group_total(jnp.concatenate([sums[:, :128], sums[:, 128:]], axis=0)) * (
        1.0 / (count * GROUP_CH)
    )
    spread = values - jnp.concatenate([means[0:1], means[1:2]], axis=1)
    squares = jnp.sum(spread * spread, axis=0, keepdims=True)
    squares = group_total(jnp.concatenate([squares[:, :128], squares[:, 128:]], axis=0))
    part = lax.broadcasted_iota(jnp.int32, (1, 128), 1) & 12
    packed = jnp.where(
        part < 8,
        jnp.where(part == 0, means[0:1], means[1:2]),
        jnp.where(part == 8, squares[0:1], squares[1:2]),
    )
    stat_row[...] = packed.reshape(1, 1, 128)

    for t in range(4):
        row_out[0, t * 8 : t * 8 + 8] = values[t * 96 : t * 96 + 8]
        row_out[1, t * 8 : t * 8 + 8] = values[t * 96 + 88 : t * 96 + 96]
    for side, cell in ((0, 0), (1, 7)):
        for half in range(2):
            lanes = slice(half * 128, half * 128 + 128)
            col_out[side, :, lanes] = own[half, pl.ds(cell, 48, stride=8), :].astype(jnp.bfloat16)
            corner_out[side, 0:4, lanes] = own[half, pl.ds(cell, 4, stride=96), :]
            corner_out[2 + side, 0:4, lanes] = own[half, pl.ds(88 + cell, 4, stride=96), :]

    @pl.when(is_root)
    def _():
        pl.semaphore_wait(barrier, 8)
        gathered[pl.ds(me, 1)] = packed.reshape(1, 1, 128)

    @pl.when(jnp.logical_not(is_root))
    def _():
        pl.semaphore_wait(barrier, 9)
        pltpu.make_async_remote_copy(
            src_ref=stat_row,
            dst_ref=gathered.at[pl.ds(me, 1)],
            send_sem=stat_send,
            recv_sem=stat_recv,
            device_id=(ROOT_ROW, ROOT_COL),
            device_id_type=MESH,
        ).start()

    halos = []
    for source, target, device in (
        (row_out.at[0], row_in.at[1], (up, col)),
        (row_out.at[1], row_in.at[0], (down, col)),
        (col_out.at[0], col_in.at[1], (row, left)),
        (col_out.at[1], col_in.at[0], (row, right)),
        (corner_out.at[0], corner_in.at[3], (up, left)),
        (corner_out.at[1], corner_in.at[2], (up, right)),
        (corner_out.at[2], corner_in.at[1], (down, left)),
        (corner_out.at[3], corner_in.at[0], (down, right)),
    ):
        copy = pltpu.make_async_remote_copy(
            src_ref=source,
            dst_ref=target,
            send_sem=halo_send.at[len(halos)],
            recv_sem=halo_recv.at[len(halos)],
            device_id=device,
            device_id_type=MESH,
        )
        copy.start()
        halos.append(copy)

    for copy in halos:
        copy.wait_recv()

    at_row = (row == 0, row == rows - 1)
    at_col = (col == 0, col == cols - 1)
    for half in range(2):
        lanes = slice(half * 128, half * 128 + 128)
        for t in range(4):
            base = 8 + t * 112
            windows[1, half, base + 8 : base + 104] = own[half, t * 96 : t * 96 + 96]
            for side, at, edge in ((0, base, 0), (1, base + 104, 88)):
                windows[1, half, at : at + 8] = jnp.where(
                    at_row[side],
                    own[half, t * 96 + edge : t * 96 + edge + 8],
                    row_in[side, t * 8 : t * 8 + 8, lanes],
                )
        for side, cell in ((0, 0), (1, 7)):
            column = jnp.where(
                at_col[side],
                own[half, pl.ds(cell, 48, stride=8), :],
                col_in[side, :, lanes].astype(F32),
            )
            for t in range(4):
                rims[side, half, t * 14 + 1 : t * 14 + 13] = column[t * 12 : t * 12 + 12]
            for end, place, inner in ((0, 0, 1), (1, 13, 12)):
                rims[side, half, pl.ds(place, 4, stride=14), :] = jnp.where(
                    at_row[end],
                    rims[side, half, pl.ds(inner, 4, stride=14), :],
                    jnp.where(
                        at_col[side],
                        windows[1, half, pl.ds(8 + place * 8 + cell, 4, stride=112), :],
                        corner_in[2 * end + side, 0:4, lanes],
                    ),
                )
        for t in range(4):
            base = 8 + t * 112
            windows[0, half, base : base + 112] = windows[1, half, base - 1 : base + 111]
            windows[2, half, base : base + 112] = windows[1, half, base + 1 : base + 113]
        windows[0, half, pl.ds(8, 56, stride=8), :] = rims[0, half, 0:56]
        windows[2, half, pl.ds(15, 56, stride=8), :] = rims[1, half, 0:56]

    for copy in later:
        copy.wait()

    plane_root = col == ROOT_COL
    fan_out = params.at[0]

    def send_params(device):
        pltpu.make_async_remote_copy(
            src_ref=fan_out,
            dst_ref=fan_out,
            send_sem=param_send,
            recv_sem=param_recv,
            device_id=device,
            device_id_type=MESH,
        ).start()

    @pl.when(is_root)
    def _():
        incoming = gathered.at[pl.ds(0, devices - 1)]
        pltpu.make_async_copy(incoming, incoming, stat_recv).wait()
        stats = gathered[...].reshape(devices, 128)
        total = jnp.sum(stats, axis=0, keepdims=True)
        mean = total * (1.0 / devices)
        shift = stats - mean
        between = jnp.sum(shift * shift, axis=0, keepdims=True)
        lane = lax.broadcasted_iota(jnp.int32, (1, 128), 1)
        per_device = float(count * GROUP_CH)
        variance = (total + per_device * pltpu.roll(between, 8, 1)) * (
            1.0 / (devices * per_device)
        )
        merged = jnp.where((lane & 8) == 0, mean, variance)
        quarters = jnp.concatenate(
            [jnp.where((lane & 15) == 4 * q, merged, 0.0) for q in range(4)], axis=0
        )
        quarters = group_total(quarters)
        for half in range(2):
            scaling = gain_ref[half : half + 1] * lax.rsqrt(
                quarters[2 + half : 3 + half] + EPSILON
            )
            params[0, half : half + 1] = scaling
            params[0, 2 + half : 3 + half] = (
                shift_ref[half : half + 1] - quarters[half : half + 1] * scaling
            )

    @pl.when(jnp.logical_not(is_root))
    def _():
        pltpu.make_async_copy(fan_out, fan_out, param_recv).wait()

    @pl.when(plane_root)
    def _():
        def beside(i, carry):
            @pl.when(i != col)
            def _():
                send_params((row, i))

            return carry

        lax.fori_loop(0, cols, beside, 0)

    @pl.when(is_root)
    def _():
        def beyond(i, carry):
            @pl.when(i != row)
            def _():
                send_params((i, col))

            return carry

        lax.fori_loop(0, rows, beyond, 0)

    for c in range(3):
        for half in range(2):
            scaling = params[0, half : half + 1]
            offsets = params[0, 2 + half : 3 + half]
            for t in range(4):
                normed = windows[c, half, 8 + t * 112 : 120 + t * 112] * scaling + offsets
                halved = 0.5 * normed
                active = halved + halved * jnp.tanh(halved)
                even = active.astype(jnp.bfloat16)
                odd = active[8:104].astype(jnp.bfloat16)
                for b, cells in enumerate((even[0:96], odd, even[16:112])):
                    tap = (3 * b + c) * 256 + half * 128
                    patches[t * 96 : t * 96 + 96, tap : tap + 128] = cells

    bias = bias_ref[...]
    depth = 9 * 256
    newest = jnp.dot(patches[...], weights[2 * depth :], preferred_element_type=F32) + bias
    middle = jnp.dot(patches[0:288], weights[depth : 2 * depth], preferred_element_type=F32)
    oldest = jnp.dot(patches[0:192], weights[0:depth], preferred_element_type=F32)
    for t in range(4):
        m, o = max(t - 1, 0) * 96, max(t - 2, 0) * 96
        out_ref[t * 96 : t * 96 + 96] = (
            newest[t * 96 : t * 96 + 96] + middle[m : m + 96] + oldest[o : o + 96]
        ).astype(jnp.bfloat16)

    for copy in halos:
        copy.wait_send()

    @pl.when(jnp.logical_not(is_root))
    def _():
        pltpu.make_async_copy(stat_row, stat_row, stat_send).wait()

    @pl.when(plane_root)
    def _():
        sent = params.at[pl.ds(0, cols - 1)]
        pltpu.make_async_copy(sent, sent, param_send).wait()

    @pl.when(is_root)
    def _():
        sent = params.at[pl.ds(0, rows - 1)]
        pltpu.make_async_copy(sent, sent, param_send).wait()


def solution(mesh):
    rows, cols = mesh.shape["row"], mesh.shape["col"]

    def body(latent, group_gain, group_shift, taps, kernel_bias):
        frames, height, breadth, channels = latent.shape
        cells = frames * height * breadth
        vmem = pl.BlockSpec(memory_space=pltpu.VMEM)
        remote = pl.BlockSpec(memory_space=pltpu.HBM)
        result = pl.pallas_call(
            functools.partial(kernel, rows, cols),
            out_shape=jax.ShapeDtypeStruct((cells, channels), jnp.bfloat16),
            in_specs=[remote] * 5,
            out_specs=vmem,
            scratch_shapes=[
                pltpu.VMEM((cells, channels), jnp.bfloat16),
                pltpu.VMEM((2, 128), F32),
                pltpu.VMEM((2, 128), F32),
                pltpu.VMEM((1, channels), F32),
                pltpu.VMEM((27 * channels, channels), jnp.bfloat16),
                pltpu.VMEM((2, cells, 128), F32),
                pltpu.VMEM((2, 32, channels), F32),
                pltpu.VMEM((2, 48, channels), jnp.bfloat16),
                pltpu.VMEM((4, 8, channels), F32),
                pltpu.VMEM((2, 32, channels), F32),
                pltpu.VMEM((2, 48, channels), jnp.bfloat16),
                pltpu.VMEM((4, 8, channels), F32),
                pltpu.VMEM((1, 1, 128), F32),
                pltpu.VMEM((rows * cols, 1, 128), F32),
                pltpu.VMEM((cols, 8, 128), F32),
                pltpu.VMEM((3, 2, 464, 128), F32),
                pltpu.VMEM((2, 2, 64, 128), F32),
                pltpu.VMEM((cells, 9 * channels), jnp.bfloat16),
                pltpu.SemaphoreType.DMA((5,)),
                pltpu.SemaphoreType.DMA((8,)),
                pltpu.SemaphoreType.DMA((8,)),
                pltpu.SemaphoreType.DMA,
                pltpu.SemaphoreType.DMA,
                pltpu.SemaphoreType.DMA,
                pltpu.SemaphoreType.DMA,
            ],
            compiler_params=pltpu.CompilerParams(
                collective_id=0, has_side_effects=True, vmem_limit_bytes=64 * 2**20
            ),
        )(
            latent.reshape(cells, channels),
            group_gain.reshape(2, 128),
            group_shift.reshape(2, 128),
            taps.reshape(27 * channels, channels),
            kernel_bias.reshape(1, channels),
        )
        return result.reshape(frames, height, breadth, channels)

    return jax.shard_map(
        body,
        mesh=mesh,
        in_specs=(P(None, "row", "col", None), P(), P(), P(), P()),
        out_specs=P(None, "row", "col", None),
        check_vma=False,
    )
```

time: 242 us -> 30.4 us (0.13)
  the two profiles are of different devices: /device:TPU:1 before, /device:TPU:37 now
where the time goes in v1:
time: 30.4 us; the launch traced here: 30.3 us
  Pallas kernels  28.6 us (94%)
  local copies, waits for them, and re-layouts  1.62 us (5%)
    pallas_call x1, Pallas kernels, body(): pl.pallas_call(functools.partial(kernel, rows, cols), out_shape=jax.Shape...  28.6 us
    unnamed x1, local copies, waits for them, and re-layouts  1.62 us

profile of v1, /device:TPU:37, one launch (start us, length us, event | category | flops | bytes accessed | tf_op | source)
XLA Modules:
  0.0 30.3 jit_solution(9120501570970465301)
XLA Ops:
  0.0 28.6 %shard_map.55 = bf16[384,256]{1,0:T(8,128)(2,1)} custom-call(bf16[384,256]{1,0:T(8,128)(2,1)} %bitcast.8, f32[2,128]{1,0:T(2,128)} %bitcast.9, f32[2,128]{1,0:T(2,128)} %bitcast.10, bf16[6912,256]{1,0:T(8,128)(2,1)} %bitcast.6, f32[1,256]{1,0:T(1,128)} %bitcast.11), custom_call_target="tpu_custom_call" | custom-call | tf_op jit(solution)/shard_map/pallas_call | solution.py:339
  28.6 1.6 %copy.7 = bf16[4,12,8,256]{3,2,1,0:T(8,128)(2,1)} copy(bf16[4,12,8,256]{3,2,1,0:T(8,128)(2,1)} %bitcast.7) | data formatting | bytes 393216

commit v2 on v1

--- a/solution.py
+++ b/solution.py
@@ -11,17 +11,36 @@
 EPSILON = 1e-06
 MESH = pl.DeviceIdType.MESH
 ROOT_ROW, ROOT_COL = 0, 1
+NEAR = 3
 F32 = jnp.float32
 
 
+def fan_out_lists(rows, cols):
+    def lateness(device):
+        z, c = device
+        return z + (c % 2 == 0) + 1.5 * (c // 8 == 3) + 1.5 * (c // 2 % 4 == 3)
+
+    near = [(z, c) for z in range(NEAR) for c in range(cols)]
+    near = [d for d in near if d != (ROOT_ROW, ROOT_COL)]
+    near.sort(key=lateness)
+    heads = [(z, ROOT_COL) for z in range(NEAR, rows)]
+    return heads[:3] + near + heads[3:], [c for c in range(cols) if c != ROOT_COL]
+
+
 def group_total(values):
-    lane = lax.broadcasted_iota(jnp.int32, values.shape, 1)
-    for step in (1, 2, 4, 8):
-        upper = (lane & step) != 0
-        values = values + jnp.where(
-            upper, pltpu.roll(values, step, 1), pltpu.roll(values, 128 - step, 1)
-        )
+    lane = lax.broadcasted_iota(jnp.int32, values.shape, 1) & 15
+    for stride in (1, 4):
+        total = values
+        for step in (stride, 2 * stride, 3 * stride):
+            total = total + jnp.where(
+                lane >= step, pltpu.roll(values, step, 1), pltpu.roll(values, 112 + step, 1)
+            )
+        values = total
     return values
+
+
+def halves(values):
+    return jnp.concatenate([values[:, :128], values[:, 128:]], axis=0)
 
 
 def kernel(
@@ -63,6 +82,7 @@
     devices = rows * cols
     me = row * cols + col
     is_root = jnp.logical_and(row == ROOT_ROW, col == ROOT_COL)
+    passes_on = jnp.logical_and(row >= NEAR, col == ROOT_COL)
     up, down = lax.rem(row + rows - 1, rows), lax.rem(row + 1, rows)
     left, right = lax.rem(col + cols - 1, cols), lax.rem(col + 1, cols)
 
@@ -78,18 +98,17 @@
     @pl.when(is_root)
     def _():
         def greet(i, carry):
-            @pl.when(i != me)
-            def _():
+            far = lax.rem(rows // 2 + jnp.where(i & 1 == 0, i >> 1, rows - ((i + 1) >> 1)), rows)
+            for c in range(cols):
+                pl.semaphore_signal(barrier, inc=1, device_id=(far, c), device_id_type=MESH)
+            return carry
+
+        lax.fori_loop(0, rows - 1, greet, 0)
+        for c in range(cols):
+            if c != ROOT_COL:
                 pl.semaphore_signal(
-                    barrier,
-                    inc=1,
-                    device_id=(lax.div(i, cols), lax.rem(i, cols)),
-                    device_id_type=MESH,
+                    barrier, inc=1, device_id=(ROOT_ROW, c), device_id_type=MESH
                 )
-
-            return carry
-
-        lax.fori_loop(0, devices, greet, 0)
 
     later = [
         pltpu.make_async_copy(source, target, load_sem.at[1 + i])
@@ -110,20 +129,29 @@
     own[0] = values[:, :128]
     own[1] = values[:, 128:]
     count = values.shape[0]
-    sums = jnp.sum(values, axis=0, keepdims=True)
-    means = group_total(jnp.concatenate([sums[:, :128], sums[:, 128:]], axis=0)) * (
-        1.0 / (count * GROUP_CH)
-    )
-    spread = values - jnp.concatenate([means[0:1], means[1:2]], axis=1)
-    squares = jnp.sum(spread * spread, axis=0, keepdims=True)
-    squares = group_total(jnp.concatenate([squares[:, :128], squares[:, 128:]], axis=0))
+    cells = float(count * GROUP_CH)
+    first = values[0:1]
+    shifted = values - first
+    sums = halves(jnp.sum(shifted, axis=0, keepdims=True))
+    squares = halves(jnp.sum(shifted * shifted, axis=0, keepdims=True))
+    squares = squares - sums * sums * (1.0 / count)
+    first = halves(first)
+    place = lax.broadcasted_iota(jnp.int32, (2, 128), 1) & 15
+    base = jnp.where(place == 0, first, 0.0)
+    for stride in (1, 4):
+        base = base + sum(pltpu.roll(base, j * stride, 1) for j in (1, 2, 3))
+    sums = sums + count * (first - base)
+    squares = squares + sums * sums * (1.0 / count)
+    totals = group_total(jnp.concatenate([sums, squares], axis=0))
+    means = base + totals[0:2] * (1.0 / cells)
+    squares = totals[2:4] - totals[0:2] * totals[0:2] * (1.0 / cells)
     part = lax.broadcasted_iota(jnp.int32, (1, 128), 1) & 12
     packed = jnp.where(
         part < 8,
         jnp.where(part == 0, means[0:1], means[1:2]),
         jnp.where(part == 8, squares[0:1], squares[1:2]),
     )
-    stat_row[...] = packed.reshape(1, 1, 128)
+    stat_row[...] = packed
 
     for t in range(4):
         row_out[0, t * 8 : t * 8 + 8] = values[t * 96 : t * 96 + 8]
@@ -138,7 +166,7 @@
     @pl.when(is_root)
     def _():
         pl.semaphore_wait(barrier, 8)
-        gathered[pl.ds(me, 1)] = packed.reshape(1, 1, 128)
+        gathered[pl.ds(me, 1)] = packed
 
     @pl.when(jnp.logical_not(is_root))
     def _():
@@ -218,7 +246,6 @@
     for copy in later:
         copy.wait()
 
-    plane_root = col == ROOT_COL
     fan_out = params.at[0]
 
     def send_params(device):
@@ -235,55 +262,42 @@
     def _():
         incoming = gathered.at[pl.ds(0, devices - 1)]
         pltpu.make_async_copy(incoming, incoming, stat_recv).wait()
-        stats = gathered[...].reshape(devices, 128)
-        total = jnp.sum(stats, axis=0, keepdims=True)
-        mean = total * (1.0 / devices)
-        shift = stats - mean
-        between = jnp.sum(shift * shift, axis=0, keepdims=True)
-        lane = lax.broadcasted_iota(jnp.int32, (1, 128), 1)
-        per_device = float(count * GROUP_CH)
-        variance = (total + per_device * pltpu.roll(between, 8, 1)) * (
-            1.0 / (devices * per_device)
+        lane = lax.broadcasted_iota(jnp.int32, (1, 128), 1) & 15
+        base = jnp.where(lane < 8, packed, 0.0)
+        shifted = gathered[...] - base
+        sums = jnp.sum(shifted, axis=0, keepdims=True)
+        between = jnp.sum(shifted * shifted, axis=0, keepdims=True)
+        between = between - sums * sums * (1.0 / devices)
+        variance = (sums + cells * pltpu.roll(between, 8, 1)) * (1.0 / (devices * cells))
+        merged = jnp.where(
+            lane < 8, base + sums * (1.0 / devices), lax.rsqrt(variance + EPSILON)
         )
-        merged = jnp.where((lane & 8) == 0, mean, variance)
-        quarters = jnp.concatenate(
-            [jnp.where((lane & 15) == 4 * q, merged, 0.0) for q in range(4)], axis=0
-        )
-        quarters = group_total(quarters)
+        spread = []
+        for q in range(4):
+            quarter = jnp.where(lane >> 2 == q, merged, 0.0)
+            spread.append(
+                quarter + sum(pltpu.roll(quarter, 4 * (j - q) % 128, 1) for j in range(4) if j != q)
+            )
         for half in range(2):
-            scaling = gain_ref[half : half + 1] * lax.rsqrt(
-                quarters[2 + half : 3 + half] + EPSILON
-            )
+            scaling = gain_ref[half : half + 1] * spread[2 + half]
             params[0, half : half + 1] = scaling
-            params[0, 2 + half : 3 + half] = (
-                shift_ref[half : half + 1] - quarters[half : half + 1] * scaling
-            )
+            params[0, 2 + half : 3 + half] = shift_ref[half : half + 1] - spread[half] * scaling
 
     @pl.when(jnp.logical_not(is_root))
     def _():
         pltpu.make_async_copy(fan_out, fan_out, param_recv).wait()
 
-    @pl.when(plane_root)
-    def _():
-        def beside(i, carry):
-            @pl.when(i != col)
-            def _():
-                send_params((row, i))
-
-            return carry
-
-        lax.fori_loop(0, cols, beside, 0)
+    first_hand, in_plane = fan_out_lists(rows, cols)
 
     @pl.when(is_root)
     def _():
-        def beyond(i, carry):
-            @pl.when(i != row)
-            def _():
-                send_params((i, col))
-
-            return carry
-
-        lax.fori_loop(0, rows, beyond, 0)
+        for device in first_hand:
+            send_params(device)
+
+    @pl.when(passes_on)
+    def _():
+        for c in in_plane:
+            send_params((row, c))
 
     for c in range(3):
         for half in range(2):
@@ -317,15 +331,15 @@
     def _():
         pltpu.make_async_copy(stat_row, stat_row, stat_send).wait()
 
-    @pl.when(plane_root)
-    def _():
-        sent = params.at[pl.ds(0, cols - 1)]
-        pltpu.make_async_copy(sent, sent, param_send).wait()
-
-    @pl.when(is_root)
-    def _():
-        sent = params.at[pl.ds(0, rows - 1)]
-        pltpu.make_async_copy(sent, sent, param_send).wait()
+    for sender, count in (
+        (is_root, len(first_hand)),
+        (passes_on, len(in_plane)),
+    ):
+
+        @pl.when(sender)
+        def _(count=count):
+            sent = params.at[pl.ds(0, count)]
+            pltpu.make_async_copy(sent, sent, param_send).wait()
 
 
 def solution(mesh):
@@ -354,9 +368,9 @@
                 pltpu.VMEM((2, 32, channels), F32),
                 pltpu.VMEM((2, 48, channels), jnp.bfloat16),
                 pltpu.VMEM((4, 8, channels), F32),
-                pltpu.VMEM((1, 1, 128), F32),
-                pltpu.VMEM((rows * cols, 1, 128), F32),
-                pltpu.VMEM((cols, 8, 128), F32),
+                pltpu.VMEM((1, 128), F32),
+                pltpu.VMEM((rows * cols, 128), F32),
+                pltpu.VMEM((max(map(len, fan_out_lists(rows, cols))), 4, 128), F32),
                 pltpu.VMEM((3, 2, 464, 128), F32),
                 pltpu.VMEM((2, 2, 64, 128), F32),
                 pltpu.VMEM((cells, 9 * channels), jnp.bfloat16),
@@ -369,14 +383,14 @@
                 pltpu.SemaphoreType.DMA,
             ],
             compiler_params=pltpu.CompilerParams(
-                collective_id=0, has_side_effects=True, vmem_limit_bytes=64 * 2**20
+                collective_id=0, has_side_effects=True, vmem_limit_bytes=48 * 2**20
             ),
         )(
-            latent.reshape(cells, channels),
-            group_gain.reshape(2, 128),
-            group_shift.reshape(2, 128),
-            taps.reshape(27 * channels, channels),
-            kernel_bias.reshape(1, channels),
+            pltpu.with_memory_space_constraint(latent.reshape(cells, channels), pltpu.HBM),
+            pltpu.with_memory_space_constraint(group_gain.reshape(2, 128), pltpu.HBM),
+            pltpu.with_memory_space_constraint(group_shift.reshape(2, 128), pltpu.HBM),
+            pltpu.with_memory_space_constraint(taps.reshape(27 * channels, channels), pltpu.HBM),
+            pltpu.with_memory_space_constraint(kernel_bias.reshape(1, channels), pltpu.HBM),
         )
         return result.reshape(frames, height, breadth, channels)
 

time: 30.4 us -> 26.8 us (0.88)
  the two profiles are of different devices: /device:TPU:37 before, /device:TPU:1 now
where the time goes in v2:
time: 26.8 us; the launch traced here: 26.4 us
  Pallas kernels  25.7 us (96%)
  local copies, waits for them, and re-layouts  0.68 us (3%)
    pallas_call x1, Pallas kernels, body(): pl.pallas_call(functools.partial(kernel, rows, cols), out_shape=jax.Shape...  25.7 us
    unnamed x1, local copies, waits for them, and re-layouts  0.68 us

profile of v2, /device:TPU:1, one launch (start us, length us, event | category | flops | bytes accessed | tf_op | source)
XLA Modules:
  0.0 26.4 jit_solution(16740702823380423718)
XLA Ops:
  0.0 25.7 %shard_map.55 = bf16[384,256]{1,0:T(8,128)(2,1)S(1)} custom-call(bf16[384,256]{1,0:T(8,128)(2,1)} %bitcast.8, f32[2,128]{1,0:T(2,128)} %bitcast.9, f32[2,128]{1,0:T(2,128)} %bitcast.10, bf16[6912,256]{1,0:T(8,128)(2,1)} %bitcast.7, f32[1,256]{1,0:T(1,128)} %bitcast.11), custom_call_target="tpu_custom_call" | custom-call | tf_op jit(solution)/shard_map/pallas_call | solution.py:353
  25.7 0.7 %copy.7 = bf16[4,12,8,256]{3,2,1,0:T(8,128)(2,1)} copy(bf16[4,12,8,256]{3,2,1,0:T(8,128)(2,1)S(1)} %bitcast.6) | data formatting | bytes 393216

commit v3 on v2

--- a/solution.py
+++ b/solution.py
@@ -12,19 +12,22 @@
 MESH = pl.DeviceIdType.MESH
 ROOT_ROW, ROOT_COL = 0, 1
 NEAR = 3
+SIDES = (64, 112)
+CORNERS = (160, 168, 176, 184)
 F32 = jnp.float32
 
 
 def fan_out_lists(rows, cols):
     def lateness(device):
         z, c = device
-        return z + (c % 2 == 0) + 1.5 * (c // 8 == 3) + 1.5 * (c // 2 % 4 == 3)
+        x, y = c // 8, c // 2 % 4
+        return (0, 2, 3)[z] + (z == 0 and max(x, y) == 3) - 0.5 * (z > 0 and x == 3)
 
     near = [(z, c) for z in range(NEAR) for c in range(cols)]
     near = [d for d in near if d != (ROOT_ROW, ROOT_COL)]
     near.sort(key=lateness)
     heads = [(z, ROOT_COL) for z in range(NEAR, rows)]
-    return heads[:3] + near + heads[3:], [c for c in range(cols) if c != ROOT_COL]
+    return heads[:4] + near[:64] + heads[4:] + near[64:], [c for c in range(cols) if c != ROOT_COL]
 
 
 def group_total(values):
@@ -53,26 +56,20 @@
     bias_hbm,
     out_ref,
     raw,
-    gain_ref,
-    shift_ref,
-    bias_ref,
+    affine,
     weights,
     own,
-    row_out,
-    col_out,
-    corner_out,
-    row_in,
-    col_in,
-    corner_in,
+    rim_out,
+    rim_in,
     stat_row,
     gathered,
-    params,
+    merged_row,
     windows,
     rims,
     patches,
     load_sem,
-    halo_send,
-    halo_recv,
+    rim_send,
+    rim_recv,
     stat_send,
     stat_recv,
     param_send,
@@ -110,19 +107,10 @@
                     barrier, inc=1, device_id=(ROOT_ROW, c), device_id_type=MESH
                 )
 
-    later = [
-        pltpu.make_async_copy(source, target, load_sem.at[1 + i])
-        for i, (source, target) in enumerate(
-            (
-                (gain_hbm, gain_ref),
-                (shift_hbm, shift_ref),
-                (bias_hbm, bias_ref),
-                (weights_hbm, weights),
-            )
-        )
-    ]
-    for copy in later:
-        copy.start()
+    for i, source in enumerate((gain_hbm, shift_hbm, bias_hbm)):
+        pltpu.make_async_copy(source, affine.at[i], load_sem.at[1]).start()
+    load_weights = pltpu.make_async_copy(weights_hbm, weights, load_sem.at[2])
+    load_weights.start()
 
     load.wait()
     values = raw[...].astype(F32)
@@ -154,14 +142,16 @@
     stat_row[...] = packed
 
     for t in range(4):
-        row_out[0, t * 8 : t * 8 + 8] = values[t * 96 : t * 96 + 8]
-        row_out[1, t * 8 : t * 8 + 8] = values[t * 96 + 88 : t * 96 + 96]
+        rim_out[t * 8 : t * 8 + 8] = values[t * 96 : t * 96 + 8]
+        rim_out[32 + t * 8 : 40 + t * 8] = values[t * 96 + 88 : t * 96 + 96]
     for side, cell in ((0, 0), (1, 7)):
         for half in range(2):
             lanes = slice(half * 128, half * 128 + 128)
-            col_out[side, :, lanes] = own[half, pl.ds(cell, 48, stride=8), :].astype(jnp.bfloat16)
-            corner_out[side, 0:4, lanes] = own[half, pl.ds(cell, 4, stride=96), :]
-            corner_out[2 + side, 0:4, lanes] = own[half, pl.ds(88 + cell, 4, stride=96), :]
+            at = SIDES[side]
+            rim_out[at : at + 48, lanes] = own[half, pl.ds(cell, 48, stride=8), :]
+            for end, place in ((0, 0), (1, 88)):
+                at = CORNERS[2 * end + side]
+                rim_out[at : at + 4, lanes] = own[half, pl.ds(place + cell, 4, stride=96), :]
 
     @pl.when(is_root)
     def _():
@@ -180,30 +170,26 @@
             device_id_type=MESH,
         ).start()
 
-    halos = []
-    for source, target, device in (
-        (row_out.at[0], row_in.at[1], (up, col)),
-        (row_out.at[1], row_in.at[0], (down, col)),
-        (col_out.at[0], col_in.at[1], (row, left)),
-        (col_out.at[1], col_in.at[0], (row, right)),
-        (corner_out.at[0], corner_in.at[3], (up, left)),
-        (corner_out.at[1], corner_in.at[2], (up, right)),
-        (corner_out.at[2], corner_in.at[1], (down, left)),
-        (corner_out.at[3], corner_in.at[0], (down, right)),
+    for source, target, size, device in (
+        (0, 32, 32, (up, col)),
+        (32, 0, 32, (down, col)),
+        (SIDES[0], SIDES[1], 48, (row, left)),
+        (SIDES[1], SIDES[0], 48, (row, right)),
+        (CORNERS[0], CORNERS[3], 8, (up, left)),
+        (CORNERS[1], CORNERS[2], 8, (up, right)),
+        (CORNERS[2], CORNERS[1], 8, (down, left)),
+        (CORNERS[3], CORNERS[0], 8, (down, right)),
     ):
-        copy = pltpu.make_async_remote_copy(
-            src_ref=source,
-            dst_ref=target,
-            send_sem=halo_send.at[len(halos)],
-            recv_sem=halo_recv.at[len(halos)],
+        pltpu.make_async_remote_copy(
+            src_ref=rim_out.at[pl.ds(source, size)],
+            dst_ref=rim_in.at[pl.ds(target, size)],
+            send_sem=rim_send,
+            recv_sem=rim_recv,
             device_id=device,
             device_id_type=MESH,
-        )
-        copy.start()
-        halos.append(copy)
-
-    for copy in halos:
-        copy.wait_recv()
+        ).start()
+
+    pltpu.make_async_copy(rim_in, rim_in, rim_recv).wait()
 
     at_row = (row == 0, row == rows - 1)
     at_col = (col == 0, col == cols - 1)
@@ -216,24 +202,25 @@
                 windows[1, half, at : at + 8] = jnp.where(
                     at_row[side],
                     own[half, t * 96 + edge : t * 96 + edge + 8],
-                    row_in[side, t * 8 : t * 8 + 8, lanes],
+                    rim_in[side * 32 + t * 8 : side * 32 + t * 8 + 8, lanes],
                 )
         for side, cell in ((0, 0), (1, 7)):
             column = jnp.where(
                 at_col[side],
                 own[half, pl.ds(cell, 48, stride=8), :],
-                col_in[side, :, lanes].astype(F32),
+                rim_in[SIDES[side] : SIDES[side] + 48, lanes],
             )
             for t in range(4):
                 rims[side, half, t * 14 + 1 : t * 14 + 13] = column[t * 12 : t * 12 + 12]
             for end, place, inner in ((0, 0, 1), (1, 13, 12)):
+                corner = CORNERS[2 * end + side]
                 rims[side, half, pl.ds(place, 4, stride=14), :] = jnp.where(
                     at_row[end],
                     rims[side, half, pl.ds(inner, 4, stride=14), :],
                     jnp.where(
                         at_col[side],
                         windows[1, half, pl.ds(8 + place * 8 + cell, 4, stride=112), :],
-                        corner_in[2 * end + side, 0:4, lanes],
+                        rim_in[corner : corner + 4, lanes],
                     ),
                 )
         for t in range(4):
@@ -243,15 +230,13 @@
         windows[0, half, pl.ds(8, 56, stride=8), :] = rims[0, half, 0:56]
         windows[2, half, pl.ds(15, 56, stride=8), :] = rims[1, half, 0:56]
 
-    for copy in later:
-        copy.wait()
-
-    fan_out = params.at[0]
+    pltpu.make_async_copy(affine, affine, load_sem.at[1]).wait()
+    load_weights.wait()
 
     def send_params(device):
         pltpu.make_async_remote_copy(
-            src_ref=fan_out,
-            dst_ref=fan_out,
+            src_ref=merged_row,
+            dst_ref=merged_row,
             send_sem=param_send,
             recv_sem=param_recv,
             device_id=device,
@@ -272,20 +257,11 @@
         merged = jnp.where(
             lane < 8, base + sums * (1.0 / devices), lax.rsqrt(variance + EPSILON)
         )
-        spread = []
-        for q in range(4):
-            quarter = jnp.where(lane >> 2 == q, merged, 0.0)
-            spread.append(
-                quarter + sum(pltpu.roll(quarter, 4 * (j - q) % 128, 1) for j in range(4) if j != q)
-            )
-        for half in range(2):
-            scaling = gain_ref[half : half + 1] * spread[2 + half]
-            params[0, half : half + 1] = scaling
-            params[0, 2 + half : 3 + half] = shift_ref[half : half + 1] - spread[half] * scaling
+        merged_row[...] = merged
 
     @pl.when(jnp.logical_not(is_root))
     def _():
-        pltpu.make_async_copy(fan_out, fan_out, param_recv).wait()
+        pltpu.make_async_copy(merged_row, merged_row, param_recv).wait()
 
     first_hand, in_plane = fan_out_lists(rows, cols)
 
@@ -299,12 +275,21 @@
         for c in in_plane:
             send_params((row, c))
 
+    merged = merged_row[...]
+    quarter = lax.broadcasted_iota(jnp.int32, (1, 128), 1) >> 2 & 3
+    spread = []
+    for q in range(4):
+        part = jnp.where(quarter == q, merged, 0.0)
+        spread.append(part + sum(pltpu.roll(part, 4 * (j - q) % 128, 1) for j in range(4) if j != q))
+    scalings = [affine[0, half : half + 1] * spread[2 + half] for half in range(2)]
+    offsets = [affine[1, half : half + 1] - spread[half] * scalings[half] for half in range(2)]
+
+    depth = 9 * 256
+    newest = middle = oldest = 0.0
     for c in range(3):
         for half in range(2):
-            scaling = params[0, half : half + 1]
-            offsets = params[0, 2 + half : 3 + half]
             for t in range(4):
-                normed = windows[c, half, 8 + t * 112 : 120 + t * 112] * scaling + offsets
+                normed = windows[c, half, 8 + t * 112 : 120 + t * 112] * scalings[half] + offsets[half]
                 halved = 0.5 * normed
                 active = halved + halved * jnp.tanh(halved)
                 even = active.astype(jnp.bfloat16)
@@ -312,20 +297,30 @@
                 for b, cells in enumerate((even[0:96], odd, even[16:112])):
                     tap = (3 * b + c) * 256 + half * 128
                     patches[t * 96 : t * 96 + 96, tap : tap + 128] = cells
-
-    bias = bias_ref[...]
-    depth = 9 * 256
-    newest = jnp.dot(patches[...], weights[2 * depth :], preferred_element_type=F32) + bias
-    middle = jnp.dot(patches[0:288], weights[depth : 2 * depth], preferred_element_type=F32)
-    oldest = jnp.dot(patches[0:192], weights[0:depth], preferred_element_type=F32)
+        for b in range(3):
+            tap = (3 * b + c) * 256
+            taps = slice(tap, tap + 256)
+            newest += jnp.dot(
+                patches[:, taps],
+                weights[2 * depth + tap : 2 * depth + tap + 256],
+                preferred_element_type=F32,
+            )
+            middle += jnp.dot(
+                patches[0:288, taps],
+                weights[depth + tap : depth + tap + 256],
+                preferred_element_type=F32,
+            )
+            oldest += jnp.dot(
+                patches[0:192, taps], weights[tap : tap + 256], preferred_element_type=F32
+            )
+    newest += jnp.concatenate([affine[2, 0:1], affine[2, 1:2]], axis=1)
     for t in range(4):
         m, o = max(t - 1, 0) * 96, max(t - 2, 0) * 96
         out_ref[t * 96 : t * 96 + 96] = (
             newest[t * 96 : t * 96 + 96] + middle[m : m + 96] + oldest[o : o + 96]
         ).astype(jnp.bfloat16)
 
-    for copy in halos:
-        copy.wait_send()
+    pltpu.make_async_copy(rim_out, rim_out, rim_send).wait()
 
     @pl.when(jnp.logical_not(is_root))
     def _():
@@ -338,7 +333,7 @@
 
         @pl.when(sender)
         def _(count=count):
-            sent = params.at[pl.ds(0, count)]
+            sent = gathered.at[pl.ds(0, count)]
             pltpu.make_async_copy(sent, sent, param_send).wait()
 
 
@@ -357,26 +352,20 @@
             out_specs=vmem,
             scratch_shapes=[
                 pltpu.VMEM((cells, channels), jnp.bfloat16),
-                pltpu.VMEM((2, 128), F32),
-                pltpu.VMEM((2, 128), F32),
-                pltpu.VMEM((1, channels), F32),
+                pltpu.VMEM((3, 2, 128), F32),
                 pltpu.VMEM((27 * channels, channels), jnp.bfloat16),
                 pltpu.VMEM((2, cells, 128), F32),
-                pltpu.VMEM((2, 32, channels), F32),
-                pltpu.VMEM((2, 48, channels), jnp.bfloat16),
-                pltpu.VMEM((4, 8, channels), F32),
-                pltpu.VMEM((2, 32, channels), F32),
-                pltpu.VMEM((2, 48, channels), jnp.bfloat16),
-                pltpu.VMEM((4, 8, channels), F32),
+                pltpu.VMEM((192, channels), F32),
+                pltpu.VMEM((192, channels), F32),
                 pltpu.VMEM((1, 128), F32),
                 pltpu.VMEM((rows * cols, 128), F32),
-                pltpu.VMEM((max(map(len, fan_out_lists(rows, cols))), 4, 128), F32),
+                pltpu.VMEM((1, 128), F32),
                 pltpu.VMEM((3, 2, 464, 128), F32),
                 pltpu.VMEM((2, 2, 64, 128), F32),
                 pltpu.VMEM((cells, 9 * channels), jnp.bfloat16),
-                pltpu.SemaphoreType.DMA((5,)),
-                pltpu.SemaphoreType.DMA((8,)),
-                pltpu.SemaphoreType.DMA((8,)),
+                pltpu.SemaphoreType.DMA((3,)),
+                pltpu.SemaphoreType.DMA,
+                pltpu.SemaphoreType.DMA,
                 pltpu.SemaphoreType.DMA,
                 pltpu.SemaphoreType.DMA,
                 pltpu.SemaphoreType.DMA,
@@ -390,7 +379,7 @@
             pltpu.with_memory_space_constraint(group_gain.reshape(2, 128), pltpu.HBM),
             pltpu.with_memory_space_constraint(group_shift.reshape(2, 128), pltpu.HBM),
             pltpu.with_memory_space_constraint(taps.reshape(27 * channels, channels), pltpu.HBM),
-            pltpu.with_memory_space_constraint(kernel_bias.reshape(1, channels), pltpu.HBM),
+            pltpu.with_memory_space_constraint(kernel_bias.reshape(2, 128), pltpu.HBM),
         )
         return result.reshape(frames, height, breadth, channels)
 

time: 26.8 us -> 25.9 us (0.966)
  Pallas kernels: 25.7 us -> 24.8 us
    pallas_call x1, Pallas kernels: 25.7 us -> 24.8 us  [body(): pl.pallas_call(functools.partial(kernel, rows, cols), out_shape=jax.Shape...]
where the time goes in v3:
time: 25.9 us; the launch traced here: 25.5 us
  Pallas kernels  24.8 us (96%)
  local copies, waits for them, and re-layouts  0.68 us (3%)
    pallas_call x1, Pallas kernels, body(): pl.pallas_call(functools.partial(kernel, rows, cols), out_shape=jax.Shape...  24.8 us
    unnamed x1, local copies, waits for them, and re-layouts  0.68 us

profile of v3, /device:TPU:1, one launch (start us, length us, event | category | flops | bytes accessed | tf_op | source)
XLA Modules:
  0.0 25.5 jit_solution(15348998585350931352)
XLA Ops:
  0.0 24.8 %shard_map.55 = bf16[384,256]{1,0:T(8,128)(2,1)S(1)} custom-call(bf16[384,256]{1,0:T(8,128)(2,1)} %bitcast.8, f32[2,128]{1,0:T(2,128)} %bitcast.9, f32[2,128]{1,0:T(2,128)} %bitcast.10, bf16[6912,256]{1,0:T(8,128)(2,1)} %bitcast.7, f32[2,128]{1,0:T(2,128)} %bitcast.11), custom_call_target="tpu_custom_call" | custom-call | tf_op jit(solution)/shard_map/pallas_call | solution.py:348
  24.9 0.7 %copy.7 = bf16[4,12,8,256]{3,2,1,0:T(8,128)(2,1)} copy(bf16[4,12,8,256]{3,2,1,0:T(8,128)(2,1)S(1)} %bitcast.6) | data formatting | bytes 393216

commit v4 on v3

--- a/solution.py
+++ b/solution.py
@@ -10,24 +10,24 @@
 GROUP_CH = 16
 EPSILON = 1e-06
 MESH = pl.DeviceIdType.MESH
-ROOT_ROW, ROOT_COL = 0, 1
-NEAR = 3
 SIDES = (64, 112)
 CORNERS = (160, 168, 176, 184)
 F32 = jnp.float32
 
 
-def fan_out_lists(rows, cols):
-    def lateness(device):
-        z, c = device
-        x, y = c // 8, c // 2 % 4
-        return (0, 2, 3)[z] + (z == 0 and max(x, y) == 3) - 0.5 * (z > 0 and x == 3)
-
-    near = [(z, c) for z in range(NEAR) for c in range(cols)]
-    near = [d for d in near if d != (ROOT_ROW, ROOT_COL)]
-    near.sort(key=lateness)
-    heads = [(z, ROOT_COL) for z in range(NEAR, rows)]
-    return heads[:4] + near[:64] + heads[4:] + near[64:], [c for c in range(cols) if c != ROOT_COL]
+SERVED = {
+    1: (0,),
+    9: (4, 8, 5, 9),
+    3: (1, 2, 6, 10),
+    25: (12, 13, 14, 15),
+    7: (3, 7, 11),
+}
+
+
+def roots_of(cols):
+    if cols == 32:
+        return SERVED
+    return {1: (), 0: tuple(range(cols // 2))}
 
 
 def group_total(values):
@@ -78,8 +78,8 @@
     row, col = lax.axis_index("row"), lax.axis_index("col")
     devices = rows * cols
     me = row * cols + col
-    is_root = jnp.logical_and(row == ROOT_ROW, col == ROOT_COL)
-    passes_on = jnp.logical_and(row >= NEAR, col == ROOT_COL)
+    served = roots_of(cols)
+    is_root = functools.reduce(jnp.logical_or, [me == r for r in served])
     up, down = lax.rem(row + rows - 1, rows), lax.rem(row + 1, rows)
     left, right = lax.rem(col + cols - 1, cols), lax.rem(col + 1, cols)
 
@@ -101,11 +101,10 @@
             return carry
 
         lax.fori_loop(0, rows - 1, greet, 0)
-        for c in range(cols):
-            if c != ROOT_COL:
-                pl.semaphore_signal(
-                    barrier, inc=1, device_id=(ROOT_ROW, c), device_id_type=MESH
-                )
+        for offset in range(1, cols):
+            pl.semaphore_signal(
+                barrier, inc=1, device_id=(0, (col + offset) & (cols - 1)), device_id_type=MESH
+            )
 
     for i, source in enumerate((gain_hbm, shift_hbm, bias_hbm)):
         pltpu.make_async_copy(source, affine.at[i], load_sem.at[1]).start()
@@ -153,22 +152,28 @@
                 at = CORNERS[2 * end + side]
                 rim_out[at : at + 4, lanes] = own[half, pl.ds(place + cell, 4, stride=96), :]
 
-    @pl.when(is_root)
-    def _():
-        pl.semaphore_wait(barrier, 8)
-        gathered[pl.ds(me, 1)] = packed
-
-    @pl.when(jnp.logical_not(is_root))
-    def _():
-        pl.semaphore_wait(barrier, 9)
+    def send_stats(c):
         pltpu.make_async_remote_copy(
             src_ref=stat_row,
             dst_ref=gathered.at[pl.ds(me, 1)],
             send_sem=stat_send,
             recv_sem=stat_recv,
-            device_id=(ROOT_ROW, ROOT_COL),
+            device_id=(0, c),
             device_id_type=MESH,
         ).start()
+
+    @pl.when(is_root)
+    def _():
+        pl.semaphore_wait(barrier, 7 + len(served))
+        gathered[pl.ds(me, 1)] = packed
+        for r in served:
+            pl.when(me != r)(functools.partial(send_stats, r))
+
+    @pl.when(jnp.logical_not(is_root))
+    def _():
+        pl.semaphore_wait(barrier, 8 + len(served))
+        for r in served:
+            send_stats(r)
 
     for source, target, size, device in (
         (0, 32, 32, (up, col)),
@@ -263,17 +268,21 @@
     def _():
         pltpu.make_async_copy(merged_row, merged_row, param_recv).wait()
 
-    first_hand, in_plane = fan_out_lists(rows, cols)
-
-    @pl.when(is_root)
-    def _():
-        for device in first_hand:
-            send_params(device)
-
-    @pl.when(passes_on)
-    def _():
-        for c in in_plane:
-            send_params((row, c))
+    def targets(r):
+        return [
+            (z, 2 * chip + core)
+            for z in range(rows)
+            for chip in served[r]
+            for core in (1, 0)
+            if z > 0 or 2 * chip + core not in served
+        ]
+
+    for r in served:
+
+        @pl.when(me == r)
+        def _(r=r):
+            for device in targets(r):
+                send_params(device)
 
     merged = merged_row[...]
     quarter = lax.broadcasted_iota(jnp.int32, (1, 128), 1) >> 2 & 3
@@ -322,19 +331,24 @@
 
     pltpu.make_async_copy(rim_out, rim_out, rim_send).wait()
 
+    def wait_rows(count, semaphore):
+        sent = gathered.at[pl.ds(0, count)]
+        pltpu.make_async_copy(sent, sent, semaphore).wait()
+
+    @pl.when(is_root)
+    def _():
+        wait_rows(len(served) - 1, stat_send)
+
     @pl.when(jnp.logical_not(is_root))
     def _():
-        pltpu.make_async_copy(stat_row, stat_row, stat_send).wait()
-
-    for sender, count in (
-        (is_root, len(first_hand)),
-        (passes_on, len(in_plane)),
-    ):
-
-        @pl.when(sender)
-        def _(count=count):
-            sent = gathered.at[pl.ds(0, count)]
-            pltpu.make_async_copy(sent, sent, param_send).wait()
+        wait_rows(len(served), stat_send)
+
+    for r in served:
+        if targets(r):
+
+            @pl.when(me == r)
+            def _(r=r):
+                wait_rows(len(targets(r)), param_send)
 
 
 def solution(mesh):

time: 25.9 us -> 25.7 us (level)
  no operation moved by 1% of the time
where the time goes in v4:
time: 25.7 us; the launch traced here: 25.6 us
  Pallas kernels  24.9 us (97%)
  local copies, waits for them, and re-layouts  0.68 us (3%)
    pallas_call x1, Pallas kernels, body(): pl.pallas_call(functools.partial(kernel, rows, cols), out_shape=jax.Shape...  24.9 us
    unnamed x1, local copies, waits for them, and re-layouts  0.68 us

profile of v4, /device:TPU:1, one launch (start us, length us, event | category | flops | bytes accessed | tf_op | source)
XLA Modules:
  0.0 25.6 jit_solution(10371563232837237233)
XLA Ops:
  0.0 24.9 %shard_map.55 = bf16[384,256]{1,0:T(8,128)(2,1)S(1)} custom-call(bf16[384,256]{1,0:T(8,128)(2,1)} %bitcast.8, f32[2,128]{1,0:T(2,128)} %bitcast.9, f32[2,128]{1,0:T(2,128)} %bitcast.10, bf16[6912,256]{1,0:T(8,128)(2,1)} %bitcast.7, f32[2,128]{1,0:T(2,128)} %bitcast.11), custom_call_target="tpu_custom_call" | custom-call | tf_op jit(solution)/shard_map/pallas_call | solution.py:362
  24.9 0.7 %copy.7 = bf16[4,12,8,256]{3,2,1,0:T(8,128)(2,1)} copy(bf16[4,12,8,256]{3,2,1,0:T(8,128)(2,1)S(1)} %bitcast.6) | data formatting | bytes 393216

commit v5 on v4

--- a/solution.py
+++ b/solution.py
@@ -83,8 +83,14 @@
     up, down = lax.rem(row + rows - 1, rows), lax.rem(row + 1, rows)
     left, right = lax.rem(col + cols - 1, cols), lax.rem(col + 1, cols)
 
-    load = pltpu.make_async_copy(latent_hbm, raw, load_sem.at[0])
-    load.start()
+    loads = [
+        pltpu.make_async_copy(
+            latent_hbm.at[pl.ds(part * 192, 192)], raw.at[pl.ds(part * 192, 192)], load_sem.at[part]
+        )
+        for part in range(2)
+    ]
+    for load in loads:
+        load.start()
 
     barrier = pltpu.get_barrier_semaphore()
     for r in (up, row, down):
@@ -107,20 +113,24 @@
             )
 
     for i, source in enumerate((gain_hbm, shift_hbm, bias_hbm)):
-        pltpu.make_async_copy(source, affine.at[i], load_sem.at[1]).start()
-    load_weights = pltpu.make_async_copy(weights_hbm, weights, load_sem.at[2])
+        pltpu.make_async_copy(source, affine.at[i], load_sem.at[2]).start()
+    load_weights = pltpu.make_async_copy(weights_hbm, weights, load_sem.at[3])
     load_weights.start()
 
-    load.wait()
-    values = raw[...].astype(F32)
-    own[0] = values[:, :128]
-    own[1] = values[:, 128:]
-    count = values.shape[0]
+    count = raw.shape[0]
     cells = float(count * GROUP_CH)
-    first = values[0:1]
-    shifted = values - first
-    sums = halves(jnp.sum(shifted, axis=0, keepdims=True))
-    squares = halves(jnp.sum(shifted * shifted, axis=0, keepdims=True))
+    loads[0].wait()
+    first = raw[0:16].astype(F32)[0:1]
+    sums = squares = 0.0
+    for part in range(2):
+        if part:
+            loads[part].wait()
+        shifted = raw[part * 192 : part * 192 + 192].astype(F32) - first
+        shifted = shifted.reshape(24, 8, shifted.shape[1])
+        sums = sums + jnp.sum(shifted, axis=0)
+        squares = squares + jnp.sum(shifted * shifted, axis=0)
+    sums = halves(jnp.sum(sums, axis=0, keepdims=True))
+    squares = halves(jnp.sum(squares, axis=0, keepdims=True))
     squares = squares - sums * sums * (1.0 / count)
     first = halves(first)
     place = lax.broadcasted_iota(jnp.int32, (2, 128), 1) & 15
@@ -140,6 +150,32 @@
     )
     stat_row[...] = packed
 
+    def send_stats(c):
+        pltpu.make_async_remote_copy(
+            src_ref=stat_row,
+            dst_ref=gathered.at[pl.ds(me, 1)],
+            send_sem=stat_send,
+            recv_sem=stat_recv,
+            device_id=(0, c),
+            device_id_type=MESH,
+        ).start()
+
+    @pl.when(is_root)
+    def _():
+        pl.semaphore_wait(barrier, 7 + len(served))
+        gathered[pl.ds(me, 1)] = packed
+        for r in served:
+            pl.when(me != r)(functools.partial(send_stats, r))
+
+    @pl.when(jnp.logical_not(is_root))
+    def _():
+        pl.semaphore_wait(barrier, 8 + len(served))
+        for r in served:
+            send_stats(r)
+
+    values = raw[...].astype(F32)
+    own[0, 0:count] = values[:, :128]
+    own[1, 0:count] = values[:, 128:]
     for t in range(4):
         rim_out[t * 8 : t * 8 + 8] = values[t * 96 : t * 96 + 8]
         rim_out[32 + t * 8 : 40 + t * 8] = values[t * 96 + 88 : t * 96 + 96]
@@ -151,29 +187,6 @@
             for end, place in ((0, 0), (1, 88)):
                 at = CORNERS[2 * end + side]
                 rim_out[at : at + 4, lanes] = own[half, pl.ds(place + cell, 4, stride=96), :]
-
-    def send_stats(c):
-        pltpu.make_async_remote_copy(
-            src_ref=stat_row,
-            dst_ref=gathered.at[pl.ds(me, 1)],
-            send_sem=stat_send,
-            recv_sem=stat_recv,
-            device_id=(0, c),
-            device_id_type=MESH,
-        ).start()
-
-    @pl.when(is_root)
-    def _():
-        pl.semaphore_wait(barrier, 7 + len(served))
-        gathered[pl.ds(me, 1)] = packed
-        for r in served:
-            pl.when(me != r)(functools.partial(send_stats, r))
-
-    @pl.when(jnp.logical_not(is_root))
-    def _():
-        pl.semaphore_wait(barrier, 8 + len(served))
-        for r in served:
-            send_stats(r)
 
     for source, target, size, device in (
         (0, 32, 32, (up, col)),
@@ -235,7 +248,7 @@
         windows[0, half, pl.ds(8, 56, stride=8), :] = rims[0, half, 0:56]
         windows[2, half, pl.ds(15, 56, stride=8), :] = rims[1, half, 0:56]
 
-    pltpu.make_async_copy(affine, affine, load_sem.at[1]).wait()
+    pltpu.make_async_copy(affine, affine, load_sem.at[2]).wait()
     load_weights.wait()
 
     def send_params(device):
@@ -254,7 +267,7 @@
         pltpu.make_async_copy(incoming, incoming, stat_recv).wait()
         lane = lax.broadcasted_iota(jnp.int32, (1, 128), 1) & 15
         base = jnp.where(lane < 8, packed, 0.0)
-        shifted = gathered[...] - base
+        shifted = gathered[0:devices] - base
         sums = jnp.sum(shifted, axis=0, keepdims=True)
         between = jnp.sum(shifted * shifted, axis=0, keepdims=True)
         between = between - sums * sums * (1.0 / devices)
@@ -368,16 +381,16 @@
                 pltpu.VMEM((cells, channels), jnp.bfloat16),
                 pltpu.VMEM((3, 2, 128), F32),
                 pltpu.VMEM((27 * channels, channels), jnp.bfloat16),
-                pltpu.VMEM((2, cells, 128), F32),
+                pltpu.VMEM((2, 768, 128), F32),
                 pltpu.VMEM((192, channels), F32),
                 pltpu.VMEM((192, channels), F32),
                 pltpu.VMEM((1, 128), F32),
-                pltpu.VMEM((rows * cols, 128), F32),
+                pltpu.VMEM((rows * cols + 8, 128), F32),
                 pltpu.VMEM((1, 128), F32),
-                pltpu.VMEM((3, 2, 464, 128), F32),
-                pltpu.VMEM((2, 2, 64, 128), F32),
+                pltpu.VMEM((3, 2, 904, 128), F32),
+                pltpu.VMEM((2, 2, 112, 128), F32),
                 pltpu.VMEM((cells, 9 * channels), jnp.bfloat16),
-                pltpu.SemaphoreType.DMA((3,)),
+                pltpu.SemaphoreType.DMA((4,)),
                 pltpu.SemaphoreType.DMA,
                 pltpu.SemaphoreType.DMA,
                 pltpu.SemaphoreType.DMA,

time: 25.7 us -> 25.7 us (level)
  no operation moved by 1% of the time
where the time goes in v5:
time: 25.7 us; the launch traced here: 25.6 us
  Pallas kernels  24.9 us (97%)
  local copies, waits for them, and re-layouts  0.68 us (3%)
    pallas_call x1, Pallas kernels, body(): pl.pallas_call(functools.partial(kernel, rows, cols), out_shape=jax.Shape...  24.9 us
    unnamed x1, local copies, waits for them, and re-layouts  0.68 us

profile of v5, /device:TPU:1, one launch (start us, length us, event | category | flops | bytes accessed | tf_op | source)
XLA Modules:
  0.0 25.6 jit_solution(4143470181491215005)
XLA Ops:
  0.0 24.9 %shard_map.55 = bf16[384,256]{1,0:T(8,128)(2,1)S(1)} custom-call(bf16[384,256]{1,0:T(8,128)(2,1)} %bitcast.8, f32[2,128]{1,0:T(2,128)} %bitcast.9, f32[2,128]{1,0:T(2,128)} %bitcast.10, bf16[6912,256]{1,0:T(8,128)(2,1)} %bitcast.7, f32[2,128]{1,0:T(2,128)} %bitcast.11), custom_call_target="tpu_custom_call" | custom-call | tf_op jit(solution)/shard_map/pallas_call | solution.py:375
  24.9 0.7 %copy.7 = bf16[4,12,8,256]{3,2,1,0:T(8,128)(2,1)} copy(bf16[4,12,8,256]{3,2,1,0:T(8,128)(2,1)S(1)} %bitcast.6) | data formatting | bytes 393216

commit v6 on v4

--- a/solution.py
+++ b/solution.py
@@ -113,9 +113,9 @@
 
     load.wait()
     values = raw[...].astype(F32)
-    own[0] = values[:, :128]
-    own[1] = values[:, 128:]
     count = values.shape[0]
+    own[0, 0:count] = values[:, :128]
+    own[1, 0:count] = values[:, 128:]
     cells = float(count * GROUP_CH)
     first = values[0:1]
     shifted = values - first
@@ -254,7 +254,7 @@
         pltpu.make_async_copy(incoming, incoming, stat_recv).wait()
         lane = lax.broadcasted_iota(jnp.int32, (1, 128), 1) & 15
         base = jnp.where(lane < 8, packed, 0.0)
-        shifted = gathered[...] - base
+        shifted = gathered[0:devices] - base
         sums = jnp.sum(shifted, axis=0, keepdims=True)
         between = jnp.sum(shifted * shifted, axis=0, keepdims=True)
         between = between - sums * sums * (1.0 / devices)
@@ -368,14 +368,14 @@
                 pltpu.VMEM((cells, channels), jnp.bfloat16),
                 pltpu.VMEM((3, 2, 128), F32),
                 pltpu.VMEM((27 * channels, channels), jnp.bfloat16),
-                pltpu.VMEM((2, cells, 128), F32),
+                pltpu.VMEM((2, 768, 128), F32),
                 pltpu.VMEM((192, channels), F32),
                 pltpu.VMEM((192, channels), F32),
                 pltpu.VMEM((1, 128), F32),
-                pltpu.VMEM((rows * cols, 128), F32),
+                pltpu.VMEM((rows * cols + 8, 128), F32),
                 pltpu.VMEM((1, 128), F32),
-                pltpu.VMEM((3, 2, 464, 128), F32),
-                pltpu.VMEM((2, 2, 64, 128), F32),
+                pltpu.VMEM((3, 2, 904, 128), F32),
+                pltpu.VMEM((2, 2, 112, 128), F32),
                 pltpu.VMEM((cells, 9 * channels), jnp.bfloat16),
                 pltpu.SemaphoreType.DMA((3,)),
                 pltpu.SemaphoreType.DMA,

time: 25.7 us -> 25.7 us (level)
  no operation moved by 1% of the time
where the time goes in v6:
time: 25.7 us; the launch traced here: 25.6 us
  Pallas kernels  24.9 us (97%)
  local copies, waits for them, and re-layouts  0.68 us (3%)
    pallas_call x1, Pallas kernels, body(): pl.pallas_call(functools.partial(kernel, rows, cols), out_shape=jax.Shape...  24.9 us
    unnamed x1, local copies, waits for them, and re-layouts  0.68 us

profile of v6, /device:TPU:1, one launch (start us, length us, event | category | flops | bytes accessed | tf_op | source)
XLA Modules:
  0.0 25.6 jit_solution(5356067514085868257)
XLA Ops:
  0.0 24.9 %shard_map.55 = bf16[384,256]{1,0:T(8,128)(2,1)S(1)} custom-call(bf16[384,256]{1,0:T(8,128)(2,1)} %bitcast.8, f32[2,128]{1,0:T(2,128)} %bitcast.9, f32[2,128]{1,0:T(2,128)} %bitcast.10, bf16[6912,256]{1,0:T(8,128)(2,1)} %bitcast.7, f32[2,128]{1,0:T(2,128)} %bitcast.11), custom_call_target="tpu_custom_call" | custom-call | tf_op jit(solution)/shard_map/pallas_call | solution.py:362
  24.9 0.7 %copy.7 = bf16[4,12,8,256]{3,2,1,0:T(8,128)(2,1)} copy(bf16[4,12,8,256]{3,2,1,0:T(8,128)(2,1)S(1)} %bitcast.6) | data formatting | bytes 393216

commit v7 on v6

--- a/solution.py
+++ b/solution.py
@@ -11,7 +11,7 @@
 EPSILON = 1e-06
 MESH = pl.DeviceIdType.MESH
 SIDES = (64, 112)
-CORNERS = (160, 168, 176, 184)
+CORNERS = (160, 176, 192, 208)
 F32 = jnp.float32
 
 
@@ -140,17 +140,21 @@
     )
     stat_row[...] = packed
 
-    for t in range(4):
-        rim_out[t * 8 : t * 8 + 8] = values[t * 96 : t * 96 + 8]
-        rim_out[32 + t * 8 : 40 + t * 8] = values[t * 96 + 88 : t * 96 + 96]
+    for end in (0, 88):
+        edge = [values[t * 96 + end : t * 96 + end + 8] for t in range(4)]
+        at = 32 * (end > 0)
+        rim_out[at : at + 32] = jnp.concatenate(edge, axis=0).astype(jnp.bfloat16)
     for side, cell in ((0, 0), (1, 7)):
         for half in range(2):
             lanes = slice(half * 128, half * 128 + 128)
             at = SIDES[side]
-            rim_out[at : at + 48, lanes] = own[half, pl.ds(cell, 48, stride=8), :]
+            rim_out[at : at + 48, lanes] = own[half, pl.ds(cell, 48, stride=8), :].astype(jnp.bfloat16)
             for end, place in ((0, 0), (1, 88)):
                 at = CORNERS[2 * end + side]
-                rim_out[at : at + 4, lanes] = own[half, pl.ds(place + cell, 4, stride=96), :]
+                corner = own[half, pl.ds(place + cell, 4, stride=96), :]
+                rim_out[at : at + 16, lanes] = jnp.concatenate(
+                    [corner, jnp.zeros((12, 128), F32)], axis=0
+                ).astype(jnp.bfloat16)
 
     def send_stats(c):
         pltpu.make_async_remote_copy(
@@ -180,10 +184,10 @@
         (32, 0, 32, (down, col)),
         (SIDES[0], SIDES[1], 48, (row, left)),
         (SIDES[1], SIDES[0], 48, (row, right)),
-        (CORNERS[0], CORNERS[3], 8, (up, left)),
-        (CORNERS[1], CORNERS[2], 8, (up, right)),
-        (CORNERS[2], CORNERS[1], 8, (down, left)),
-        (CORNERS[3], CORNERS[0], 8, (down, right)),
+        (CORNERS[0], CORNERS[3], 16, (up, left)),
+        (CORNERS[1], CORNERS[2], 16, (up, right)),
+        (CORNERS[2], CORNERS[1], 16, (down, left)),
+        (CORNERS[3], CORNERS[0], 16, (down, right)),
     ):
         pltpu.make_async_remote_copy(
             src_ref=rim_out.at[pl.ds(source, size)],
@@ -207,13 +211,13 @@
                 windows[1, half, at : at + 8] = jnp.where(
                     at_row[side],
                     own[half, t * 96 + edge : t * 96 + edge + 8],
-                    rim_in[side * 32 + t * 8 : side * 32 + t * 8 + 8, lanes],
+                    rim_in[side * 32 : side * 32 + 32, lanes].astype(F32)[t * 8 : t * 8 + 8],
                 )
         for side, cell in ((0, 0), (1, 7)):
             column = jnp.where(
                 at_col[side],
                 own[half, pl.ds(cell, 48, stride=8), :],
-                rim_in[SIDES[side] : SIDES[side] + 48, lanes],
+                rim_in[SIDES[side] : SIDES[side] + 48, lanes].astype(F32),
             )
             for t in range(4):
                 rims[side, half, t * 14 + 1 : t * 14 + 13] = column[t * 12 : t * 12 + 12]
@@ -225,7 +229,7 @@
                     jnp.where(
                         at_col[side],
                         windows[1, half, pl.ds(8 + place * 8 + cell, 4, stride=112), :],
-                        rim_in[corner : corner + 4, lanes],
+                        rim_in[corner : corner + 16, lanes].astype(F32)[0:4],
                     ),
                 )
         for t in range(4):
@@ -369,8 +373,8 @@
                 pltpu.VMEM((3, 2, 128), F32),
                 pltpu.VMEM((27 * channels, channels), jnp.bfloat16),
                 pltpu.VMEM((2, 768, 128), F32),
-                pltpu.VMEM((192, channels), F32),
-                pltpu.VMEM((192, channels), F32),
+                pltpu.VMEM((224, channels), jnp.bfloat16),
+                pltpu.VMEM((224, channels), jnp.bfloat16),
                 pltpu.VMEM((1, 128), F32),
                 pltpu.VMEM((rows * cols + 8, 128), F32),
                 pltpu.VMEM((1, 128), F32),

time: 25.7 us -> 25.7 us (level)
  no operation moved by 1% of the time
where the time goes in v7:
time: 25.7 us; the launch traced here: 25.6 us
  Pallas kernels  24.9 us (97%)
  local copies, waits for them, and re-layouts  0.68 us (3%)
    pallas_call x1, Pallas kernels, body(): pl.pallas_call(functools.partial(kernel, rows, cols), out_shape=jax.Shape...  24.9 us
    unnamed x1, local copies, waits for them, and re-layouts  0.68 us

profile of v7, /device:TPU:1, one launch (start us, length us, event | category | flops | bytes accessed | tf_op | source)
XLA Modules:
  0.0 25.6 jit_solution(22847805920076780)
XLA Ops:
  0.0 24.9 %shard_map.55 = bf16[384,256]{1,0:T(8,128)(2,1)S(1)} custom-call(bf16[384,256]{1,0:T(8,128)(2,1)} %bitcast.8, f32[2,128]{1,0:T(2,128)} %bitcast.9, f32[2,128]{1,0:T(2,128)} %bitcast.10, bf16[6912,256]{1,0:T(8,128)(2,1)} %bitcast.7, f32[2,128]{1,0:T(2,128)} %bitcast.11), custom_call_target="tpu_custom_call" | custom-call | tf_op jit(solution)/shard_map/pallas_call | solution.py:366
  24.9 0.7 %copy.7 = bf16[4,12,8,256]{3,2,1,0:T(8,128)(2,1)} copy(bf16[4,12,8,256]{3,2,1,0:T(8,128)(2,1)S(1)} %bitcast.6) | data formatting | bytes 393216
